TPU v7x, 128 devices: a whole 4x4x4 slice. The times are simulated.
128 devices in a mesh: grp: 8 (over z, core), leaf: 16 (over x, y).
Axes of the slice: x: 4, y: 4, z: 4, core: 2. Of those that a mesh axis runs over, the one named last changes fastest.
Arguments:
- points: float32 [524288, 64], P(('grp', 'leaf')), may hold values from -6 to 6
- rhs: float32 [524288, 128], P(('grp', 'leaf')), may hold values from -6 to 6
- leaf_basis: float32 [2048, 256, 128], P(('grp', 'leaf')), may hold values from -0.375 to 0.375
- leaf_skeleton: int32 [2048, 128], P(('grp', 'leaf')), may hold values from 0 to 255, as said below
- node_basis: float32 [128, 2048, 128], P(('grp', 'leaf')), may hold values from -0.125 to 0.125
- node_skeleton: int32 [128, 128], P(('grp', 'leaf')), may hold values from 0 to 2047, as said below
- group_basis: float32 [8, 2048, 128], P('grp', 'leaf'), may hold values from -0.125 to 0.125
- group_skeleton: int32 [8, 128], P('grp'), may hold values from 0 to 2047, as said below
- near_live: int32 [2048, 9], P(('grp', 'leaf')), may hold values from 0 to 1, as said below
Outputs:
- product: float32 [524288, 128], P(('grp', 'leaf'))
Inputs may be any that keep to these rules, and one draw needn't show every extreme that they name: `leaf_skeleton`: the indices of one row are distinct. `node_skeleton`: the indices of one row are distinct. `group_skeleton`: the indices of one row are distinct. `near_live`: column 4 is 1 everywhere; entries whose leaf lies outside the row's coarse node are 0; the share of live tiles differs from device to device.
All inputs are finite; a program needn't handle non-finite values.
Results may differ from a plain program's by a relative error of at most 0.0003.
Values sent between devices are 32-bit elements; how exact they have to be, the bound alone decides.
A program may use at most 128 MiB of HBM per device.

v0:
```python
import jax
import jax.numpy as jnp
from jax import lax
from jax.sharding import PartitionSpec as P

NEAR = 4


highest = lax.Precision.HIGHEST


def with_halo(block, sides, width):
    for axis, dim in sides:
        count = lax.axis_size(axis)
        forward = [(i, i + 1) for i in range(count - 1)]
        backward = [(target, source) for source, target in forward]
        low = lax.ppermute(
            lax.slice_in_dim(block, block.shape[dim] - width, None, axis=dim), axis, forward
        )
        high = lax.ppermute(lax.slice_in_dim(block, 0, width, axis=dim), axis, backward)
        block = jnp.concatenate([low, block, high], axis=dim)
    return block


def kernel(left_pts, right_pts):
    distance = (
        jnp.sum(left_pts * left_pts, axis=1)[:, None]
        + jnp.sum(right_pts * right_pts, axis=1)[None, :]
        - 2.0 * jnp.dot(left_pts, right_pts.T, precision=highest)
    )
    return jnp.exp(distance * (-2.0 / left_pts.shape[1]))


def pick(source_table, indices):
    return source_table[indices]


def near_scan(source_rows, shift, targets, alive_table, offsets, leaf_size, width):
    window = alive_table.shape[1] * leaf_size

    def near_leaf(carried, inputs):
        target, alive_flags, offset = inputs
        window_rows = lax.dynamic_slice_in_dim(source_rows, (offset + shift) * leaf_size, window, 0)
        column_mask = jnp.repeat(alive_flags.astype(jnp.float32), leaf_size)
        kernel_block = kernel(target, window_rows[:, :width]) * column_mask[None, :]
        return (carried, jnp.dot(kernel_block, window_rows[:, width:], precision=highest))

    unused, result = lax.scan(near_leaf, jnp.zeros((), jnp.int32), (targets, alive_table, offsets))
    return result


def per_device(
    points,
    rhs,
    leaf_basis,
    leaf_skeleton,
    node_basis,
    node_skeleton,
    group_basis,
    group_skeleton,
    near_live,
):
    leaf_count, leaf_size, rank_size = leaf_basis.shape
    width = points.shape[1]
    columns = rhs.shape[1]
    leaf_points = points.reshape(leaf_count, leaf_size, width)
    leaf_rhs = rhs.reshape(leaf_count, leaf_size, columns)
    leaf_coef = jnp.einsum("lpr,lpc->lrc", leaf_basis, leaf_rhs, precision=highest)
    node_coef = jnp.einsum(
        "kr,kc->rc",
        node_basis[0],
        leaf_coef.reshape(leaf_count * rank_size, columns),
        precision=highest,
    )
    leaf_pts = jax.vmap(pick)(leaf_points, leaf_skeleton)
    node_pts = leaf_pts.reshape(leaf_count * rank_size, width)[node_skeleton[0]]
    position = lax.axis_index("leaf")
    group_part = jnp.einsum("kr,kc->rc", group_basis[0], node_coef, precision=highest)
    local_index = group_skeleton[0] - position * rank_size
    inside = (local_index >= 0) & (local_index < rank_size)
    pts_part = jnp.where(inside[:, None], node_pts[jnp.clip(local_index, 0, rank_size - 1)], 0.0)
    far_pts = lax.all_gather(node_pts[None], "leaf", axis=0, tiled=True)
    far_coef = lax.all_gather(node_coef[None], "leaf", axis=0, tiled=True)
    blocks = jax.vmap(kernel, (None, 0))(node_pts, far_pts)
    source = jnp.arange(far_pts.shape[0], dtype=jnp.int32)
    weights = (jnp.abs(source - position) >= 2).astype(jnp.float32)
    far_field = jnp.einsum("k,krs,ksc->rc", weights, blocks, far_coef, precision=highest)
    groups = lax.axis_size("grp")
    group_id = lax.axis_index("grp")
    group_mask = (jnp.arange(groups, dtype=jnp.int32) != group_id).astype(jnp.float32)
    group_pts, group_coef = lax.psum((pts_part, group_part), "leaf")
    every_pts, every_coef = (
        lax.all_gather(group_pts[None], "grp", axis=0, tiled=True),
        lax.all_gather(group_coef[None], "grp", axis=0, tiled=True),
    )
    blocks = jax.vmap(kernel, (None, 0))(group_pts, every_pts)
    group_field = jnp.einsum("g,grs,gsc->rc", group_mask, blocks, every_coef, precision=highest)
    node_field = far_field + jnp.dot(group_basis[0], group_field, precision=highest)
    leaf_field = jnp.dot(node_basis[0], node_field, precision=highest).reshape(
        leaf_count, rank_size, columns
    )
    far_out = jnp.einsum("lpr,lrc->lpc", leaf_basis, leaf_field, precision=highest)
    packed = jnp.concatenate([points, rhs], axis=1)
    offsets_all = jnp.arange(leaf_count, dtype=jnp.int32)
    extended = with_halo(packed, (("leaf", 0),), NEAR * leaf_size)
    near_out = near_scan(extended, 0, leaf_points, near_live, offsets_all, leaf_size, width)
    return (near_out + far_out).reshape(leaf_count * leaf_size, columns)


def solution(mesh):
    return jax.shard_map(
        per_device,
        mesh=mesh,
        in_specs=(
            P(("grp", "leaf"), None),
            P(("grp", "leaf"), None),
            P(("grp", "leaf"), None, None),
            P(("grp", "leaf"), None),
            P(("grp", "leaf"), None, None),
            P(("grp", "leaf"), None),
            P("grp", "leaf", None),
            P("grp", None),
            P(("grp", "leaf"), None),
        ),
        out_specs=P(("grp", "leaf"), None),
        check_vma=False,
    )
```

profile of v0, /device:TPU:1, one launch (start us, length us, event | category | flops | bytes accessed | tf_op | source)
XLA Modules:
  0.0 497.2 jit_solution(7327122706947328393)
XLA Ops:
  8.1 5.3 %fusion.49 = f32[16,128,128]{2,1,0:T(8,128)S(1)} fusion(f32[16,256,128]{2,1,0:T(8,128)S(1)} %copy-done, f32[16,256,128]{2,1,0:T(8,128)} %bitcast.146), kind=kOutput, calls=%fused_computation.78 | convolution fusion | flops 805306368 | bytes 5242880 | tf_op jit(solution)/shard_map/lpr,lpc->lrc/dot_general | solution.py:68
  16.2 3.0 copy.33
  19.3 2.6 pad_maximum_fusion.2
  23.3 5.6 %collective-permute-start = (f32[1024,192]{0,1:T(8,128)}, f32[1024,192]{0,1:T(8,128)}, u32[]{:S(2)}, u32[]{:S(2)}) collective-permute-start(f32[1024,192]{0,1:T(8,128)} %get-tuple-element.62), channel_id=1, source_target_pairs={{0,1},{1,2},{2,3},{3,4},{4,5},{5,6},{6,7},{7,8},{8,9},{9,10},{10,1... | collective-permute-start | bytes 2359304 | tf_op jit(solution)/shard_map/ppermute | solution.py:17
  28.8 1.9 copy.32
  30.9 30.3 %gather_fusion.2 = f32[2048,64]{1,0:T(8,128)} fusion(f32[16,256,64]{2,1,0:T(8,128)} %bitcast.142, s32[2048]{0:T(1024)S(1)} %fusion.46), kind=kCustom, calls=%fused_computation.2 | custom fusion | bytes 1064960 | tf_op jit(solution)/shard_map/vmap()/gather | solution.py:35
  63.1 23.7 %all-gather = f32[2048,64]{1,0:T(8,128)} all-gather(f32[128,64]{1,0:T(8,128)S(1)} %gather_fusion), channel_id=2, replica_groups=mesh['grp'=8,'leaf'=16] {'leaf'}, dimensions={0}, use_global_device_ids=true | all-gather | bytes 557056 | tf_op jit(solution)/shard_map/all_gather | solution.py:82
  87.7 58.7 %psum.14 = f32[128,64]{0,1:T(8,128)S(1)} all-reduce(f32[128,64]{0,1:T(8,128)S(1)} %broadcast_select_fusion), channel_id=1, replica_groups=mesh['grp'=8,'leaf'=16] {'leaf'}, use_global_device_ids=true, to_apply=%region_6.7 | all-reduce | flops 8192 | bytes 65536 | tf_op jit(solution)/shard_map/psum | solution.py:91
  146.4 33.2 %all-gather.2 = f32[1024,64]{0,1:T(8,128)S(1)} all-gather(f32[128,64]{0,1:T(8,128)S(1)} %psum.14), channel_id=4, replica_groups=mesh['grp'=8,'leaf'=16] {'grp'}, dimensions={0}, use_global_device_ids=true | all-gather | bytes 294912 | tf_op jit(solution)/shard_map/all_gather | solution.py:93
  181.3 2.3 copy.36
  183.6 2.4 copy.48
  187.1 3.2 fusion.22
  191.2 13.3 %all_gather.15 = f32[8,128,128]{2,1,0:T(8,128)S(1)} all-gather(f32[1,128,128]{2,1,0:T(8,128)S(1)} %copy.41), channel_id=1, replica_groups=mesh['grp'=8,'leaf'=16] {'grp'}, dimensions={0}, use_global_device_ids=true | all-gather | bytes 589824 | tf_op jit(solution)/shard_map/all_gather | solution.py:94
  206.2 4.7 pad_maximum_fusion
  210.9 266.2 %while.10 = (s32[]{:T(128)}, f32[16,256,128]{1,2,0:T(8,128)}, f32[16,256,64]{2,1,0:T(8,128)}, s32[16]{0:T(128)S(1)}, f32[6144,192]{0,1:T(8,128)}, /*index=5*/s32...) while((s32[]{:T(128)}, f32[16,256,128]{1,2,0:T(8,128)}, ...), condition=%wide.region_3.4_spmd, body=%wide.region_0.0_spmd.sunk | while | flops 1362228736 | bytes 9822531 | solution.py:48
  212.0 1.9 constant_dynamic-slice_fusion.3
  217.6 4.9 fusion.78
  222.5 5.1 %fusion.79 = f32[16,256,128]{1,2,0:T(8,128)} fusion(f32[16,256,128]{1,2,0:T(8,128)} %get-tuple-element.113, s32[]{:T(128)S(6)} %copy.76, f32[256,2304]{1,0:T(8,128)} %fusion.78, f32[6144,192]{0,1:T(8,128)} %get-tuple-element.127, s32[]{:T(128)S(6)} %select_n.53, s32[]{:T(128)S(6)} %add.139), kind=kOutput, calls=%fused_computation.12.clone.1 | convolution fusion | flops 905969664 | bytes 3670028 | tf_op jit(solution)/shard_map/while/body/eval_jaxpr/dot_general | solution.py:46
  228.7 1.9 constant_dynamic-slice_fusion.3
  234.2 4.9 fusion.78
  239.1 5.1 %fusion.79 = f32[16,256,128]{1,2,0:T(8,128)} fusion(f32[16,256,128]{1,2,0:T(8,128)} %get-tuple-element.113, s32[]{:T(128)S(6)} %copy.76, f32[256,2304]{1,0:T(8,128)} %fusion.78, f32[6144,192]{0,1:T(8,128)} %get-tuple-element.127, s32[]{:T(128)S(6)} %select_n.53, s32[]{:T(128)S(6)} %add.139), kind=kOutput, calls=%fused_computation.12.clone.1 | convolution fusion | flops 905969664 | bytes 3670028 | tf_op jit(solution)/shard_map/while/body/eval_jaxpr/dot_general | solution.py:46
  245.3 1.9 constant_dynamic-slice_fusion.3
  250.8 4.9 fusion.78
  255.7 5.1 %fusion.79 = f32[16,256,128]{1,2,0:T(8,128)} fusion(f32[16,256,128]{1,2,0:T(8,128)} %get-tuple-element.113, s32[]{:T(128)S(6)} %copy.76, f32[256,2304]{1,0:T(8,128)} %fusion.78, f32[6144,192]{0,1:T(8,128)} %get-tuple-element.127, s32[]{:T(128)S(6)} %select_n.53, s32[]{:T(128)S(6)} %add.139), kind=kOutput, calls=%fused_computation.12.clone.1 | convolution fusion | flops 905969664 | bytes 3670028 | tf_op jit(solution)/shard_map/while/body/eval_jaxpr/dot_general | solution.py:46
  261.9 1.9 constant_dynamic-slice_fusion.3
  267.5 4.9 fusion.78
  272.4 5.1 %fusion.79 = f32[16,256,128]{1,2,0:T(8,128)} fusion(f32[16,256,128]{1,2,0:T(8,128)} %get-tuple-element.113, s32[]{:T(128)S(6)} %copy.76, f32[256,2304]{1,0:T(8,128)} %fusion.78, f32[6144,192]{0,1:T(8,128)} %get-tuple-element.127, s32[]{:T(128)S(6)} %select_n.53, s32[]{:T(128)S(6)} %add.139), kind=kOutput, calls=%fused_computation.12.clone.1 | convolution fusion | flops 905969664 | bytes 3670028 | tf_op jit(solution)/shard_map/while/body/eval_jaxpr/dot_general | solution.py:46
  278.6 1.9 constant_dynamic-slice_fusion.3
  284.1 4.9 fusion.78
  289.0 5.1 %fusion.79 = f32[16,256,128]{1,2,0:T(8,128)} fusion(f32[16,256,128]{1,2,0:T(8,128)} %get-tuple-element.113, s32[]{:T(128)S(6)} %copy.76, f32[256,2304]{1,0:T(8,128)} %fusion.78, f32[6144,192]{0,1:T(8,128)} %get-tuple-element.127, s32[]{:T(128)S(6)} %select_n.53, s32[]{:T(128)S(6)} %add.139), kind=kOutput, calls=%fused_computation.12.clone.1 | convolution fusion | flops 905969664 | bytes 3670028 | tf_op jit(solution)/shard_map/while/body/eval_jaxpr/dot_general | solution.py:46
  295.2 1.9 constant_dynamic-slice_fusion.3
  300.7 4.9 fusion.78
  305.7 5.1 %fusion.79 = f32[16,256,128]{1,2,0:T(8,128)} fusion(f32[16,256,128]{1,2,0:T(8,128)} %get-tuple-element.113, s32[]{:T(128)S(6)} %copy.76, f32[256,2304]{1,0:T(8,128)} %fusion.78, f32[6144,192]{0,1:T(8,128)} %get-tuple-element.127, s32[]{:T(128)S(6)} %select_n.53, s32[]{:T(128)S(6)} %add.139), kind=kOutput, calls=%fused_computation.12.clone.1 | convolution fusion | flops 905969664 | bytes 3670028 | tf_op jit(solution)/shard_map/while/body/eval_jaxpr/dot_general | solution.py:46
  311.9 1.9 constant_dynamic-slice_fusion.3
  317.4 4.9 fusion.78
  322.3 5.1 %fusion.79 = f32[16,256,128]{1,2,0:T(8,128)} fusion(f32[16,256,128]{1,2,0:T(8,128)} %get-tuple-element.113, s32[]{:T(128)S(6)} %copy.76, f32[256,2304]{1,0:T(8,128)} %fusion.78, f32[6144,192]{0,1:T(8,128)} %get-tuple-element.127, s32[]{:T(128)S(6)} %select_n.53, s32[]{:T(128)S(6)} %add.139), kind=kOutput, calls=%fused_computation.12.clone.1 | convolution fusion | flops 905969664 | bytes 3670028 | tf_op jit(solution)/shard_map/while/body/eval_jaxpr/dot_general | solution.py:46
  328.5 1.9 constant_dynamic-slice_fusion.3
  334.0 4.9 fusion.78
  338.9 5.1 %fusion.79 = f32[16,256,128]{1,2,0:T(8,128)} fusion(f32[16,256,128]{1,2,0:T(8,128)} %get-tuple-element.113, s32[]{:T(128)S(6)} %copy.76, f32[256,2304]{1,0:T(8,128)} %fusion.78, f32[6144,192]{0,1:T(8,128)} %get-tuple-element.127, s32[]{:T(128)S(6)} %select_n.53, s32[]{:T(128)S(6)} %add.139), kind=kOutput, calls=%fused_computation.12.clone.1 | convolution fusion | flops 905969664 | bytes 3670028 | tf_op jit(solution)/shard_map/while/body/eval_jaxpr/dot_general | solution.py:46
  345.1 1.9 constant_dynamic-slice_fusion.3
  350.7 4.9 fusion.78
  355.6 5.1 %fusion.79 = f32[16,256,128]{1,2,0:T(8,128)} fusion(f32[16,256,128]{1,2,0:T(8,128)} %get-tuple-element.113, s32[]{:T(128)S(6)} %copy.76, f32[256,2304]{1,0:T(8,128)} %fusion.78, f32[6144,192]{0,1:T(8,128)} %get-tuple-element.127, s32[]{:T(128)S(6)} %select_n.53, s32[]{:T(128)S(6)} %add.139), kind=kOutput, calls=%fused_computation.12.clone.1 | convolution fusion | flops 905969664 | bytes 3670028 | tf_op jit(solution)/shard_map/while/body/eval_jaxpr/dot_general | solution.py:46
  361.8 1.9 constant_dynamic-slice_fusion.3
  367.3 4.9 fusion.78
  372.2 5.1 %fusion.79 = f32[16,256,128]{1,2,0:T(8,128)} fusion(f32[16,256,128]{1,2,0:T(8,128)} %get-tuple-element.113, s32[]{:T(128)S(6)} %copy.76, f32[256,2304]{1,0:T(8,128)} %fusion.78, f32[6144,192]{0,1:T(8,128)} %get-tuple-element.127, s32[]{:T(128)S(6)} %select_n.53, s32[]{:T(128)S(6)} %add.139), kind=kOutput, calls=%fused_computation.12.clone.1 | convolution fusion | flops 905969664 | bytes 3670028 | tf_op jit(solution)/shard_map/while/body/eval_jaxpr/dot_general | solution.py:46
  378.4 1.9 constant_dynamic-slice_fusion.3
  383.9 4.9 fusion.78
  388.9 5.1 %fusion.79 = f32[16,256,128]{1,2,0:T(8,128)} fusion(f32[16,256,128]{1,2,0:T(8,128)} %get-tuple-element.113, s32[]{:T(128)S(6)} %copy.76, f32[256,2304]{1,0:T(8,128)} %fusion.78, f32[6144,192]{0,1:T(8,128)} %get-tuple-element.127, s32[]{:T(128)S(6)} %select_n.53, s32[]{:T(128)S(6)} %add.139), kind=kOutput, calls=%fused_computation.12.clone.1 | convolution fusion | flops 905969664 | bytes 3670028 | tf_op jit(solution)/shard_map/while/body/eval_jaxpr/dot_general | solution.py:46
  395.1 1.9 constant_dynamic-slice_fusion.3
  400.6 4.9 fusion.78
  405.5 5.1 %fusion.79 = f32[16,256,128]{1,2,0:T(8,128)} fusion(f32[16,256,128]{1,2,0:T(8,128)} %get-tuple-element.113, s32[]{:T(128)S(6)} %copy.76, f32[256,2304]{1,0:T(8,128)} %fusion.78, f32[6144,192]{0,1:T(8,128)} %get-tuple-element.127, s32[]{:T(128)S(6)} %select_n.53, s32[]{:T(128)S(6)} %add.139), kind=kOutput, calls=%fused_computation.12.clone.1 | convolution fusion | flops 905969664 | bytes 3670028 | tf_op jit(solution)/shard_map/while/body/eval_jaxpr/dot_general | solution.py:46
  411.7 1.9 constant_dynamic-slice_fusion.3
  417.2 4.9 fusion.78
  422.1 5.1 %fusion.79 = f32[16,256,128]{1,2,0:T(8,128)} fusion(f32[16,256,128]{1,2,0:T(8,128)} %get-tuple-element.113, s32[]{:T(128)S(6)} %copy.76, f32[256,2304]{1,0:T(8,128)} %fusion.78, f32[6144,192]{0,1:T(8,128)} %get-tuple-element.127, s32[]{:T(128)S(6)} %select_n.53, s32[]{:T(128)S(6)} %add.139), kind=kOutput, calls=%fused_computation.12.clone.1 | convolution fusion | flops 905969664 | bytes 3670028 | tf_op jit(solution)/shard_map/while/body/eval_jaxpr/dot_general | solution.py:46
  433.9 4.9 fusion.78
  438.8 5.1 %fusion.79 = f32[16,256,128]{1,2,0:T(8,128)} fusion(f32[16,256,128]{1,2,0:T(8,128)} %get-tuple-element.113, s32[]{:T(128)S(6)} %copy.76, f32[256,2304]{1,0:T(8,128)} %fusion.78, f32[6144,192]{0,1:T(8,128)} %get-tuple-element.127, s32[]{:T(128)S(6)} %select_n.53, s32[]{:T(128)S(6)} %add.139), kind=kOutput, calls=%fused_computation.12.clone.1 | convolution fusion | flops 905969664 | bytes 3670028 | tf_op jit(solution)/shard_map/while/body/eval_jaxpr/dot_general | solution.py:46
  450.5 4.9 fusion.78
  455.4 5.1 %fusion.79 = f32[16,256,128]{1,2,0:T(8,128)} fusion(f32[16,256,128]{1,2,0:T(8,128)} %get-tuple-element.113, s32[]{:T(128)S(6)} %copy.76, f32[256,2304]{1,0:T(8,128)} %fusion.78, f32[6144,192]{0,1:T(8,128)} %get-tuple-element.127, s32[]{:T(128)S(6)} %select_n.53, s32[]{:T(128)S(6)} %add.139), kind=kOutput, calls=%fused_computation.12.clone.1 | convolution fusion | flops 905969664 | bytes 3670028 | tf_op jit(solution)/shard_map/while/body/eval_jaxpr/dot_general | solution.py:46
  467.1 4.9 fusion.78
  472.1 5.1 %fusion.79 = f32[16,256,128]{1,2,0:T(8,128)} fusion(f32[16,256,128]{1,2,0:T(8,128)} %get-tuple-element.113, s32[]{:T(128)S(6)} %copy.76, f32[256,2304]{1,0:T(8,128)} %fusion.78, f32[6144,192]{0,1:T(8,128)} %get-tuple-element.127, s32[]{:T(128)S(6)} %select_n.53, s32[]{:T(128)S(6)} %add.139), kind=kOutput, calls=%fused_computation.12.clone.1 | convolution fusion | flops 905969664 | bytes 3670028 | tf_op jit(solution)/shard_map/while/body/eval_jaxpr/dot_general | solution.py:46
  477.2 2.7 copy.50
  479.8 2.7 convolution_bitcast_fusion.4
  483.8 2.0 fusion.29
  487.4 2.9 copy.45
  (173 shorter events, 88.9 us)
Async XLA Ops:
  6.5 1.6 copy-start
  6.5 183.7 %all-reduce.2.cloned.1.call-start = ((), (), s32[]{:S(2)}) async-start(), calls=%async_computation | async-start | bytes 131072 | tf_op jit(solution)/shard_map/psum | solution.py:91
  8.1 5.3 %copy-start.2 = (f32[1,2048,128]{2,1,0:T(8,128)S(1)}, f32[1,2048,128]{2,1,0:T(8,128)}, u32[]{:S(2)}) copy-start(f32[1,2048,128]{2,1,0:T(8,128)} %param.15) | copy-start | bytes 3145732
  13.4 1.9 copy-start.6
  15.3 4.0 copy-start.5
  16.2 3.1 copy-start.1
  16.2 461.0 %all-gather.5.cloned.1.call-start = ((), (), s32[]{:S(2)}) async-start(), calls=%async_computation.1 | async-start | bytes 1114112 | tf_op jit(solution)/shard_map/all_gather | solution.py:83
  21.8 9.0 %copy-start.8 = (s32[16,128]{1,0:T(8,128)S(1)}, s32[16,128]{1,0:T(8,128)}, u32[]{:S(2)}) copy-start(s32[16,128]{1,0:T(8,128)} %param.14) | copy-start | bytes 24580
  21.8 9.0 %copy-start.9 = (s32[1,128]{1,0:T(1,128)S(1)}, s32[1,128]{1,0:T(1,128)}, u32[]{:S(2)}) copy-start(s32[1,128]{1,0:T(1,128)} %param.16) | copy-start | bytes 1540
  21.8 184.4 %collective-permute-start.1 = (f32[1024,192]{0,1:T(8,128)}, f32[1024,192]{0,1:T(8,128)}, u32[]{:S(2)}, u32[]{:S(2)}) collective-permute-start(f32[1024,192]{0,1:T(8,128)} %get-tuple-element.63), channel_id=1, source_target_pairs={{1,0},{2,1},{3,2},{4,3},{5,4},{6,5},{7,6},{8,7},{9,8},{10,9},{11,1... | collective-permute-start | bytes 2359304 | tf_op jit(solution)/shard_map/ppermute | solution.py:20
  23.3 183.0 %collective-permute-start = (f32[1024,192]{0,1:T(8,128)}, f32[1024,192]{0,1:T(8,128)}, u32[]{:S(2)}, u32[]{:S(2)}) collective-permute-start(f32[1024,192]{0,1:T(8,128)} %get-tuple-element.62), channel_id=1, source_target_pairs={{0,1},{1,2},{2,3},{3,4},{4,5},{5,6},{6,7},{7,8},{8,9},{9,10},{10,1... | collective-permute-start | bytes 2359304 | tf_op jit(solution)/shard_map/ppermute | solution.py:17
  30.8 56.1 %copy-start.10 = (s32[1,128]{1,0:T(1,128)S(1)}, s32[1,128]{1,0:T(1,128)}, u32[]{:S(2)}) copy-start(s32[1,128]{1,0:T(1,128)} %param.18) | copy-start | bytes 1540
  477.2 5.3 %copy-start.7 = (f32[1,128,128]{2,1,0:T(8,128)S(1)}, f32[1,128,128]{2,1,0:T(8,128)}, u32[]{:S(2)}) copy-start(f32[1,128,128]{2,1,0:T(8,128)} %param.17) | copy-start | bytes 196612
  477.2 5.6 %copy-start.3 = (f32[1,2048,128]{2,1,0:T(8,128)S(1)}, f32[1,2048,128]{2,1,0:T(8,128)}, u32[]{:S(2)}) copy-start(f32[1,2048,128]{2,1,0:T(8,128)} %param.15) | copy-start | bytes 3145732
  483.8 2.0 copy-start.4
Sparse Core Ops, SparseCore 0:
  16.3 82.5 all-reduce.1
  101.3 42.8 all-gather.4
where the time goes:
time: 501 us; the launch traced here: 497 us
  matrix products  180 us (36%)
  blocking collectives  129 us (26%)
  local copies, waits for them, and re-layouts  114 us (23%)
  other arithmetic  43.5 us (9%)
  between operations  13.7 us (3%)
  loops' own time  9.27 us (2%)
  starting transfers between devices  7.02 us (1%)
    dot_general x18, matrix products, kernel(): jnp.dot(left_pts, right_pts.T, precision=highest)  83.3 us
    dot_general x16, matrix products, near_leaf(): jnp.dot(kernel_block, window_rows[:, width:], precision=highest)  81.5 us
    psum x1, blocking collectives, per_device(): group_pts, group_coef = lax.psum((pts_part, group_part), 'leaf')  58.7 us
    while x32, local copies, waits for them, and re-layouts  53.5 us
    all_gather x1, blocking collectives, per_device(): lax.all_gather(group_pts[None], 'grp', axis=0, tiled=True)  33.2 us
    gather x1, local copies, waits for them, and re-layouts, pick(): return source_table[indices]  30.3 us
    all_gather x1, blocking collectives, per_device(): far_pts = lax.all_gather(node_pts[None], 'leaf', axis=0, tiled=True)  23.7 us
    reduce_sum x18, other arithmetic, kernel(): jnp.sum(left_pts * left_pts, axis=1)[:, None]  16.3 us
  transfers between devices with their start and end apart: 4, of which 0 were waited for; matrix products, arithmetic and copies ran while one was open for 63% of the time, Pallas kernels for 0%

commit v1 on v0

v1 whole, which is shorter than its diff:
```python
import functools
import math

import jax
import jax.numpy as jnp
from jax import lax
from jax.experimental import pallas as pl
from jax.experimental.pallas import tpu as pltpu
from jax.sharding import PartitionSpec as P

MESH = pl.DeviceIdType.MESH
f32 = jnp.float32
bf16 = jnp.bfloat16
NT = (((1,), (1,)), ((), ()))
TN = (((0,), (0,)), ((), ()))

D = 64
NRHS = 128
LEAF = 256
RANK = 128
NEAR = 4
LD = 16
ROWS = LD * LEAF
N_GRP = 8
N_LEAF = 16
SIDE = 4
ALPHA = math.sqrt(4.0 / D * math.log2(math.e))
DEAD = -32768.0
NORM_U, NORM_V, MASK = 64, 67, 70


def dot(a, b):
    return jnp.dot(a, b, preferred_element_type=f32)


def split(x):
    high = x.astype(bf16)
    return high, (x - high.astype(f32)).astype(bf16)


def halves(x):
    return x[:, :128] + x[:, 128:]


def mm3(a, b):
    a_high, a_low = split(a)
    b_high, b_low = split(b)
    row = jnp.concatenate([b_high, b_low], axis=1)
    return halves(dot(jnp.concatenate([a_high, a_low], axis=1), jnp.concatenate([row, row], axis=0)))


def lanes(shape):
    return lax.broadcasted_iota(jnp.int32, shape, 1)


def twice(packed):
    low = lanes(packed.shape) < D
    other = pltpu.roll(packed, D, 1)
    return jnp.concatenate([jnp.where(low, packed, other), jnp.where(low, other, packed)], axis=0)


def pack(doubled):
    half = doubled.shape[0] // 2
    top = doubled[:half]
    return jnp.where(lanes(top.shape) < D, top, doubled[half:])


def base_u():
    lane = lanes((1, 128))
    return ((lane >= NORM_V) & (lane < NORM_V + 3)).astype(f32)


def base_v():
    lane = lanes((1, 128))
    return ((lane >= NORM_U) & (lane < NORM_U + 3)).astype(f32)


def features(doubled, u_row, v_row):
    scaled = doubled * ALPHA
    high = scaled.astype(bf16).astype(f32)
    low = (scaled - high).astype(bf16).astype(f32)
    both = high + low
    norm = -0.25 * jnp.sum(both * both, axis=1, keepdims=True)
    n1 = norm.astype(bf16).astype(f32)
    n2 = (norm - n1).astype(bf16).astype(f32)
    n3 = norm - n1 - n2
    lane = lanes(doubled.shape)
    first = lane < D
    u = v = None
    if u_row is not None:
        extra = jnp.where(lane == NORM_U, n1, jnp.where(lane == NORM_U + 1, n2, jnp.where(lane == NORM_U + 2, n3, u_row)))
        u = jnp.concatenate([jnp.where(first, high, low), jnp.where(first, high, extra)], axis=1).astype(bf16)
    if v_row is not None:
        extra = jnp.where(lane == NORM_V, n1, jnp.where(lane == NORM_V + 1, n2, jnp.where(lane == NORM_V + 2, n3, v_row)))
        v = jnp.concatenate([high, jnp.where(first, low, extra)], axis=1).astype(bf16)
    return u, v


def kernel_block(u, v):
    return split(jnp.exp2(lax.dot_general(u, v, NT, preferred_element_type=f32)))


def apply_block(k_high, k_low, r):
    return halves(dot(k_high, r)) + dot(k_low, r[:, :128])


def body(
    points, rhs, leaf_basis, node_basis, group_basis, leaf_skel, node_skel, group_skel, live,
    out,
    pts, rh, lb, nb, gb, U, V, R, WW, acc, bias, wr, pk,
    npts, npk, gpart, gsum, gfull, gpk, gall, gct, ctp, gcs, gc, ft, fmine,
    halo_p, halo_r, src_p, tgt_p, src_c, part, fr, coef,
    in_sem, out_sem, hs_p, hr_p, hs_r, hr_r, xs_p, xr_p, ys_p, yr_p, xs_c, xr_c, ys_f, yr_f,
    s1, r1, s2, r2, s3, r3, s4, r4, s5, r5, s6, r6,
):
    g = lax.axis_index("grp")
    l = lax.axis_index("leaf")
    x = l // SIDE
    y = lax.rem(l, SIDE)

    def leaf_peer(k):
        return lax.rem(l + k, N_LEAF)

    def grp_peer(k):
        return lax.rem(g + k, N_GRP)

    def x_peer(k):
        return lax.rem(x + k, SIDE) * SIDE + y

    def y_peer(k):
        return x * SIDE + lax.rem(y + k, SIDE)

    barrier = pltpu.get_barrier_semaphore()
    for k in range(1, N_LEAF):
        pl.semaphore_signal(barrier, inc=1, device_id=(g, leaf_peer(k)), device_id_type=MESH)
    for k in range(1, N_GRP):
        pl.semaphore_signal(barrier, inc=1, device_id=(grp_peer(k), l), device_id_type=MESH)

    loads = [
        pltpu.make_async_copy(src, dst, in_sem.at[i])
        for i, (src, dst) in enumerate(
            ((points, pts), (rhs, rh), (node_basis, nb), (leaf_basis, lb), (group_basis, gb))
        )
    ]
    for load in loads:
        load.start()

    row_id = lax.broadcasted_iota(jnp.int32, (LD, 128), 0)
    column = lax.broadcasted_iota(jnp.int32, (LD, 128), 1)
    table = jnp.zeros((LD, 128), f32)
    alive = live[...].astype(f32)
    for j in range(2 * NEAR + 1):
        dead = (1.0 - alive[:, j : j + 1]) * DEAD
        table = jnp.where(column == row_id + (MASK + j), dead, table)
    bias[...] = table + base_u()

    def one_hot(s):
        return base_v() + (lanes((1, 128)) == MASK + s).astype(f32)

    def own_features(t):
        rows = pl.ds(pl.multiple_of(t * LEAF, LEAF), LEAF)
        value = pts[rows, :]
        doubled = jnp.concatenate([value, value], axis=1)
        u, v = features(doubled, bias[pl.ds(t, 1), :], one_hot(t + NEAR))
        U[rows, :] = u
        V[pl.ds(pl.multiple_of((t + NEAR) * LEAF, LEAF), LEAF), :] = v
        return doubled

    loads[0].wait()

    def edge(i, carry):
        t = jnp.where(i < NEAR, i, i + LD - 2 * NEAR)
        pk[i] = pack(own_features(t))
        return carry

    lax.fori_loop(0, 2 * NEAR, edge, 0)

    def pick(r, carry):
        index = node_skel[0, r]
        leaf = index // RANK
        row = leaf * LEAF + leaf_skel[leaf, lax.rem(index, RANK)]
        npts[pl.ds(r, 1), :] = pts[pl.ds(row, 1), :]
        return carry

    lax.fori_loop(0, RANK, pick, 0, unroll=8)
    value = npts[...]
    npk[...] = pack(jnp.concatenate([value, value], axis=1))

    def pick_group(r, carry):
        index = group_skel[0, r]
        inside = (index // RANK == l).astype(f32)
        gpart[pl.ds(r, 1), :] = npts[pl.ds(lax.rem(index, RANK), 1), :] * inside
        return carry

    lax.fori_loop(0, RANK, pick_group, 0, unroll=8)
    value = gpart[...]
    gsum[...] = jnp.concatenate([value, value], axis=1)

    pl.semaphore_wait(barrier, N_LEAF + N_GRP - 2)

    sends = []

    def send(src, dst, send_sem, recv_sem, device):
        copy = pltpu.make_async_remote_copy(
            src_ref=src, dst_ref=dst, send_sem=send_sem, recv_sem=recv_sem, device_id=device, device_id_type=MESH
        )
        copy.start()
        sends.append(copy)
        return copy

    def to_leaf(src_of, dst_of, send_sem, recv_sem):
        return [
            send(src_of(leaf_peer(k)), dst_of(k), send_sem.at[k - 1], recv_sem.at[k - 1], (g, leaf_peer(k)))
            for k in range(1, N_LEAF)
        ]

    def to_grp(src, dst, send_sem, recv_sem):
        return [
            send(src, dst, send_sem.at[k - 1], recv_sem.at[k - 1], (grp_peer(k), l)) for k in range(1, N_GRP)
        ]

    def to_x(src, dst, send_sem, recv_sem):
        return [send(src, dst, send_sem.at[k - 1], recv_sem.at[k - 1], (g, x_peer(k))) for k in range(1, SIDE)]

    def eight(i):
        return pl.ds(pl.multiple_of(i * 8, 8), 8)

    sum_pts = to_leaf(lambda p: gsum.at[eight(p)], lambda k: gct.at[k - 1], s1, r1)
    x_pts = to_x(npk, src_p.at[x], xs_p, xr_p)
    y_pts = [
        send(npk, tgt_p.at[y], ys_p.at[k - 1], yr_p.at[k - 1], (g, y_peer(k))) for k in range(1, SIDE)
    ]
    src_p[x] = npk[...]
    tgt_p[y] = npk[...]
    halo = {}
    for c in range(NEAR):
        for side, (slot, leaf, device) in enumerate(
            ((2 * NEAR - 1 - c, LD - 1 - c, leaf_peer(1)), (c, c, leaf_peer(N_LEAF - 1)))
        ):
            halo[side, c] = (
                send(pk.at[slot], halo_p.at[side, c], hs_p.at[side, c], hr_p.at[side, c], (g, device)),
                send(
                    rhs.at[pl.ds(leaf * LEAF, LEAF)], halo_r.at[side, c], hs_r.at[side, c], hr_r.at[side, c], (g, device)
                ),
            )

    loads[1].wait()
    loads[2].wait()
    loads[3].wait()
    loads[4].wait()
    wr[...] = jnp.zeros((256, 256), f32)

    def up(t, carry):
        rows = pl.ds(pl.multiple_of(t * LEAF, LEAF), LEAF)
        r_high, r_low = split(rh[rows, :])
        r = jnp.concatenate([r_high, r_low], axis=1)
        R[pl.ds(pl.multiple_of((t + NEAR) * LEAF, LEAF), LEAF), :] = r
        w = mm3(lb[rows, :], nb[pl.ds(pl.multiple_of(t * RANK, RANK), RANK), :])
        w_high, w_low = split(w)
        w = jnp.concatenate([w_high, w_low], axis=1)
        WW[rows, :] = w
        wr[...] += lax.dot_general(w, r, TN, preferred_element_type=f32)
        return carry

    lax.fori_loop(0, LD, up, 0)
    node_coef = halves(wr[0:128, :] + wr[128:256, :])
    coef[...] = node_coef
    x_coef = to_x(coef, src_c.at[x], xs_c, xr_c)
    src_c[x] = node_coef
    ctp[...] = mm3(node_coef.T, gb[...])
    sum_coef = to_leaf(lambda p: ctp.at[eight(p)], lambda k: gcs.at[k - 1], s2, r2)

    def middle(t, carry):
        own_features(t)
        return carry

    lax.fori_loop(NEAR, LD - NEAR, middle, 0)

    def tiles(t, count, s):
        rows = pl.ds(pl.multiple_of(t * LEAF, LEAF), count * LEAF)
        source = pl.ds(pl.multiple_of((s + NEAR) * LEAF, LEAF), LEAF)
        k_high, k_low = kernel_block(U[rows, :], V[source, :])
        acc[rows, :] += apply_block(k_high, k_low, R[source, :])

    def full(i, carry):
        b = i // 6
        tiles(b * 4, 4, b * 4 - 1 + lax.rem(i, 6))
        return carry

    def left(b):
        for c in range(1, NEAR):
            tiles(b * 4, NEAR - c, b * 4 - 1 - c)

    def right(b):
        for c in range(1, NEAR):
            tiles(b * 4 + c, NEAR - c, b * 4 + 4 + c)

    def partial(j, carry):
        left(j + 1)
        right(j)
        return carry

    acc[...] = jnp.zeros((ROWS, NRHS), f32)
    lax.fori_loop(1, 4, full, 0)

    for copy in sum_pts:
        copy.wait_recv()
    total = gsum[eight(l), :]
    for k in range(N_LEAF - 1):
        total = total + gct[k]
    gpart8 = eight(l)
    gfull[gpart8, :] = total
    full_pts = to_leaf(lambda p: gfull.at[gpart8], lambda k: gfull.at[gpart8], s3, r3)

    lax.fori_loop(4, 7, full, 0)

    for copy in sum_coef:
        copy.wait_recv()
    total = ctp[eight(l), :]
    for k in range(N_LEAF - 1):
        total = total + gcs[k]
    fmine[0] = total
    gc_out = to_grp(fmine.at[0], gc.at[g], s4, r4)
    gc[g] = jnp.zeros((8, 128), f32)
    for copy in full_pts:
        copy.wait_recv()
    gpk[...] = pack(gfull[...])
    all_pts = to_grp(gpk, gall.at[g], s5, r5)
    gall[g] = gpk[...]

    for copy in x_pts + y_pts + x_coef:
        copy.wait_recv()
    lane = lanes((1, 128))
    us, vs, rs = [], [], []
    for i in range(SIDE):
        u_row = base_u()
        for j in range(SIDE):
            close = jnp.abs(SIDE * x + i - SIDE * j - y) < 2
            u_row = u_row + jnp.where(lane == MASK + j, jnp.where(close, DEAD, 0.0), 0.0)
        us.append(features(twice(tgt_p[i]), u_row, None)[0])
        vs.append(features(twice(src_p[i]), None, one_hot(i))[1])
        rs.append(jnp.concatenate(split(src_c[i]), axis=1))
    k_high, k_low = kernel_block(jnp.concatenate(us, axis=0), jnp.concatenate(vs, axis=0))
    field = apply_block(k_high, k_low, jnp.concatenate(rs, axis=0))
    for i in range(SIDE):
        part[i] = field[i * 128 : (i + 1) * 128]
    y_field = [
        send(part.at[lax.rem(y + k, SIDE)], fr.at[k - 1], ys_f.at[k - 1], yr_f.at[k - 1], (g, y_peer(k)))
        for k in range(1, SIDE)
    ]

    lax.fori_loop(7, 13, full, 0)

    for copy in gc_out + all_pts:
        copy.wait_recv()
    u_own = features(twice(gpk[...]), base_u(), None)[0]
    v_all = jnp.concatenate([features(twice(gall[h]), None, base_v())[1] for h in range(N_GRP)], axis=0)
    k_high, k_low = kernel_block(v_all, u_own)
    columns = jnp.concatenate([gc[h] for h in range(N_GRP)], axis=1)
    c_high = columns.astype(bf16)
    c_low = (columns - c_high.astype(f32)).astype(bf16)
    mine = halves(
        dot(c_high, jnp.concatenate([k_high, k_low], axis=1)) + dot(c_low, jnp.concatenate([k_high, k_low], axis=1))
    )
    ft[eight(l), :] = mine
    field_out = to_leaf(lambda p: ft.at[eight(l)], lambda k: ft.at[eight(l)], s6, r6)

    lax.fori_loop(13, 23, full, 0)
    lax.fori_loop(0, 3, partial, 0)

    for c in range(NEAR):
        for side in range(2):
            for copy in halo[side, c]:
                copy.wait_recv()
            s = -1 - c if side == 0 else LD + c
            where = pl.ds((s + NEAR) * LEAF, LEAF)
            V[where, :] = features(twice(halo_p[side, c]), None, one_hot(s + NEAR))[1]
            R[where, :] = jnp.concatenate(split(halo_r[side, c]), axis=1)
            tiles(0 if side == 0 else LD - NEAR + c, NEAR - c, s)

    for copy in y_field + field_out:
        copy.wait_recv()
    node_field = part[y] + fr[0] + fr[1] + fr[2] + mm3(gb[...], ft[...].T)
    row = jnp.concatenate(split(node_field), axis=1)
    both = jnp.concatenate([row, row], axis=0)
    stores = []
    for i in range(4):
        rows = pl.ds(i * 1024, 1024)
        acc[rows, :] += halves(dot(WW[rows, :], both))
        store = pltpu.make_async_copy(acc.at[rows], out.at[rows], out_sem.at[i])
        store.start()
        stores.append(store)
    for copy in sends:
        copy.wait_send()
    for store in stores:
        store.wait()


def per_device(
    points, rhs, leaf_basis, leaf_skeleton, node_basis, node_skeleton, group_basis, group_skeleton, near_live
):
    any_ = pl.BlockSpec(memory_space=pl.ANY)
    smem = pl.BlockSpec(memory_space=pltpu.SMEM)
    vmem = pl.BlockSpec(memory_space=pltpu.VMEM)
    dma = pltpu.SemaphoreType.DMA
    V = pltpu.VMEM
    scratch = [
        V((ROWS, D), f32), V((ROWS, NRHS), f32), V((ROWS, RANK), f32), V((LD * RANK, RANK), f32), V((RANK, RANK), f32),
        V((ROWS, 256), bf16), V((ROWS + 2 * NEAR * LEAF, 256), bf16), V((ROWS + 2 * NEAR * LEAF, 256), bf16),
        V((ROWS, 256), bf16), V((ROWS, NRHS), f32), V((LD, 128), f32), V((256, 256), f32), V((2 * NEAR, 128, 128), f32),
        V((RANK, D), f32), V((64, 128), f32), V((RANK, D), f32), V((RANK, 128), f32), V((RANK, 128), f32),
        V((64, 128), f32), V((N_GRP, 64, 128), f32), V((N_LEAF - 1, 8, 128), f32), V((128, 128), f32),
        V((N_LEAF - 1, 8, 128), f32), V((N_GRP, 8, 128), f32), V((128, 128), f32), V((1, 8, 128), f32),
        V((2, NEAR, 128, 128), f32), V((2, NEAR, LEAF, 128), f32), V((SIDE, 64, 128), f32), V((SIDE, 64, 128), f32),
        V((SIDE, 128, 128), f32), V((SIDE, 128, 128), f32), V((SIDE - 1, 128, 128), f32), V((128, 128), f32),
        dma((5,)), dma((4,)), dma((2, NEAR)), dma((2, NEAR)), dma((2, NEAR)), dma((2, NEAR)),
        dma((3,)), dma((3,)), dma((3,)), dma((3,)), dma((3,)), dma((3,)), dma((3,)), dma((3,)),
        dma((15,)), dma((15,)), dma((15,)), dma((15,)), dma((15,)), dma((15,)),
        dma((7,)), dma((7,)), dma((7,)), dma((7,)), dma((15,)), dma((15,)),
    ]
    return pl.pallas_call(
        body,
        out_shape=jax.ShapeDtypeStruct((ROWS, NRHS), f32),
        in_specs=[any_, any_, any_, any_, any_, smem, smem, smem, vmem],
        out_specs=any_,
        scratch_shapes=scratch,
        compiler_params=pltpu.CompilerParams(
            collective_id=0, has_side_effects=True, vmem_limit_bytes=56 * 1024 * 1024
        ),
    )(
        points, rhs, leaf_basis.reshape(ROWS, RANK), node_basis.reshape(LD * RANK, RANK), group_basis.reshape(RANK, RANK),
        leaf_skeleton, node_skeleton, group_skeleton, near_live,
    )


def solution(mesh):
    return jax.shard_map(
        per_device,
        mesh=mesh,
        in_specs=(
            P(("grp", "leaf"), None),
            P(("grp", "leaf"), None),
            P(("grp", "leaf"), None, None),
            P(("grp", "leaf"), None),
            P(("grp", "leaf"), None, None),
            P(("grp", "leaf"), None),
            P("grp", "leaf", None),
            P("grp", None),
            P(("grp", "leaf"), None),
        ),
        out_specs=P(("grp", "leaf"), None),
        check_vma=False,
    )
```

time: 501 us -> 76.5 us (0.15)
  matrix products: 180 us -> 0 us
  blocking collectives: 129 us -> 0 us
  local copies, waits for them, and re-layouts: 114 us -> 6.2 us
  Pallas kernels: 0 us -> 70.1 us
  other arithmetic: 43.5 us -> 0 us
  between operations: 13.7 us -> 0.01 us
  loops' own time: 9.27 us -> 0 us
  starting transfers between devices: 7.02 us -> 0 us
    dot_general x42 -> x0, matrix products: 180 us -> none  [the longest x18 83.3 us: kernel(): jnp.dot(left_pts, right_pts.T, precision=highest)]
    all_gather x3 -> x0, blocking collectives: 70.3 us -> none  [the longest x1 33.2 us: per_device(): lax.all_gather(group_pts[None], 'grp', axis=0, tiled=True)]
    pallas_call x0 -> x1, Pallas kernels: none -> 70.1 us  [per_device(): pl.pallas_call(body, out_shape=jax.ShapeDtypeStruct((ROWS, NRHS), f32), i...]
    psum x1 -> x0, blocking collectives: 58.7 us -> none  [per_device(): group_pts, group_coef = lax.psum((pts_part, group_part), 'leaf')]
    while x32 -> x0, local copies, waits for them, and re-layouts: 53.5 us -> none
    gather x4 -> x0, local copies, waits for them, and re-layouts: 32.9 us -> none  [the longest x1 30.3 us: pick(): return source_table[indices]]
    reduce_sum x36 -> x0, other arithmetic: 23.5 us -> none  [the longest x18 16.3 us: kernel(): jnp.sum(left_pts * left_pts, axis=1)[:, None]]
    convert_element_type x16 -> x0, other arithmetic: 11.1 us -> none  [near_leaf(): column_mask = jnp.repeat(alive_flags.astype(jnp.float32), leaf_size)]
  transfers between devices with their start and end apart: 4 -> 0, of which waited for: 0 -> 0; matrix products, arithmetic and copies ran while one was open for 63% -> 0% of each run, Pallas kernels for 0% -> 0%
where the time goes in v1:
time: 76.5 us; the launch traced here: 76.3 us
  Pallas kernels  70.1 us (92%)
  local copies, waits for them, and re-layouts  6.2 us (8%)
    pallas_call x1, Pallas kernels, per_device(): pl.pallas_call(body, out_shape=jax.ShapeDtypeStruct((ROWS, NRHS), f32), i...  70.1 us
    unnamed x2, local copies, waits for them, and re-layouts  6.2 us

profile of v1, /device:TPU:1, one launch (start us, length us, event | category | flops | bytes accessed | tf_op | source)
XLA Modules:
  0.0 76.3 jit_solution(4151812369975397144)
XLA Ops:
  0.0 3.2 %copy.10.points = f32[4096,64]{1,0:T(8,128)} copy(f32[4096,64]{0,1:T(8,128)} %param.9) | data formatting | bytes 2097152 | tf_op args[0]
  3.2 70.1 %shard_map.91 = f32[4096,128]{1,0:T(8,128)} custom-call(f32[4096,64]{1,0:T(8,128)} %copy.10.points, f32[4096,128]{1,0:T(8,128)} %rhs.1, f32[4096,128]{1,0:T(8,128)} %bitcast.3, f32[2048,128]{1,0:T(8,128)} %bitcast.4, f32[128,128]{1,0:T(8,128)} %bitcast.5, s32[16,128]{1,0:T(8,128)} %leaf_skel.1, s32[1,128]{1,0:T(1,128)} %node_skel.1, s32[1,128]{1,0:T(1,128)} %group_skel.1, ...), custom_call_target="tpu_custom_call" | custom-call | tf_op jit(solution)/shard_map/pallas_call | solution.py:421
  73.2 3.0 %copy.12 = f32[4096,128]{1,0:T(8,128)} copy(f32[4096,128]{1,0:T(8,128)} %shard_map.91) | data formatting | bytes 4194304

commit v2 on v1

v2 whole, which is shorter than its diff:
```python
import functools
import math

import jax
import jax.numpy as jnp
from jax import lax
from jax.experimental import pallas as pl
from jax.experimental.pallas import tpu as pltpu
from jax.sharding import PartitionSpec as P

MESH = pl.DeviceIdType.MESH
f32 = jnp.float32
bf16 = jnp.bfloat16
NT = (((1,), (1,)), ((), ()))

D = 64
NRHS = 128
LEAF = 256
RANK = 128
NEAR = 4
LD = 16
ROWS = LD * LEAF
N_GRP = 8
N_LEAF = 16
SIDE = 4
ALPHA = math.sqrt(4.0 / D * math.log2(math.e))
DEAD = -32768.0
MASK = 8
PAD = NEAR * LEAF


def dot(a, b):
    return jnp.dot(a, b, preferred_element_type=f32)


def split(x):
    high = x.astype(bf16)
    return high, (x - high.astype(f32)).astype(bf16)


def pieces(x):
    high = x.astype(bf16)
    rest = x - high.astype(f32)
    middle = rest.astype(bf16)
    return jnp.concatenate([high, middle, (rest - middle.astype(f32)).astype(bf16)], axis=0)


def thirds(x):
    n = x.shape[0] // 3
    return x[:n] + x[n : 2 * n] + x[2 * n :]


def halves(x):
    return x[:, :128] + x[:, 128:]


def mm3(a, b):
    a_high, a_low = split(a)
    b_high, b_low = split(b)
    row = jnp.concatenate([b_high, b_low], axis=1)
    return halves(dot(jnp.concatenate([a_high, a_low], axis=1), jnp.concatenate([row, row], axis=0)))


def rows_of(shape):
    return lax.broadcasted_iota(jnp.int32, shape, 0)


def base_u():
    row = rows_of((D, 1))
    return ((row >= 3) & (row < 6)).astype(f32)


def base_v():
    return (rows_of((D, 1)) < 3).astype(f32)


def one_hot(s):
    return base_v() + (rows_of((D, 1)) == MASK + s).astype(f32)


def features(coordinates, u_col, v_col):
    n = coordinates.shape[1]
    scaled = coordinates * ALPHA
    high = scaled.astype(bf16)
    low = (scaled - high.astype(f32)).astype(bf16)
    both = high.astype(f32) + low.astype(f32)
    norm = -0.5 * jnp.sum(both * both, axis=0, keepdims=True)
    n1 = norm.astype(bf16).astype(f32)
    n2 = (norm - n1).astype(bf16).astype(f32)
    n3 = norm - n1 - n2
    row = rows_of((8, n))
    result = []
    for first, col, blocks in ((0, u_col, (high, low, high)), (3, v_col, (high, high, low))):
        if col is None:
            result.append(None)
            continue
        top = jnp.where(
            row == first, n1, jnp.where(row == first + 1, n2, jnp.where(row == first + 2, n3, col[:8]))
        )
        extra = jnp.concatenate([top, jnp.broadcast_to(col[8:], (D - 8, n))], axis=0).astype(bf16)
        result.append(jnp.concatenate([*blocks, extra], axis=0))
    return result


def flip(x, eye):
    return lax.dot_general(eye, x, NT, preferred_element_type=f32).astype(bf16)


def kernel_block(u, v):
    return split(jnp.exp2(dot(u, v)))


def apply_block(k_high, k_low, r):
    return halves(dot(k_high, r)) + dot(k_low, r[:, :128])


def mask_table(alive, shift):
    shape = (D, 128)
    row = rows_of(shape)
    leaf = lax.broadcasted_iota(jnp.int32, shape, 1)
    table = jnp.where((row >= MASK) & (row < MASK + LD + 2 * NEAR), DEAD, 0.0)
    for j in range(2 * NEAR + 1):
        here = (row == leaf + (MASK + j + shift)) & (row >= MASK)
        table = jnp.where(here, (1.0 - alive[j : j + 1, :]) * DEAD, table)
    return table + base_u()


def column(table, t):
    lane = lax.broadcasted_iota(jnp.int32, table.shape, 1)
    return jnp.sum(jnp.where(lane == t, table, 0.0), axis=1, keepdims=True)


def body(
    points, rhs, leaf_basis, node_basis, group_basis, leaf_skel, node_skel, group_skel, live,
    out,
    pts, rh, lb, nb, gb, U, VT, R, WW, acc, bias, wr, lt, flat,
    px, ty, gpy, py, gall, coef, src_c, ctp, gcs, gc, fmine, ft, part, fr,
    hp, hl, hr, UH, accH, hpart,
    in_sem, out_sem, xs1, xr1, ys1, yr1, ys2, yr2, xs3, xr3, ys4, yr4,
    gs1, gr1, gs2, gr2, s1, r1, s2, r2, hs1, hr1, hs2, hr2, hs3, hr3, hs4, hr4,
):
    g = lax.axis_index("grp")
    l = lax.axis_index("leaf")
    x = l // SIDE
    y = lax.rem(l, SIDE)

    def leaf_peer(k):
        return lax.rem(l + k, N_LEAF)

    def grp_peer(k):
        return lax.rem(g + k, N_GRP)

    def x_peer(k):
        return lax.rem(x + k, SIDE) * SIDE + y

    def y_peer(k):
        return x * SIDE + lax.rem(y + k, SIDE)

    barrier = pltpu.get_barrier_semaphore()
    for k in range(1, N_LEAF):
        pl.semaphore_signal(barrier, inc=1, device_id=(g, leaf_peer(k)), device_id_type=MESH)
    for k in range(1, N_GRP):
        pl.semaphore_signal(barrier, inc=1, device_id=(grp_peer(k), l), device_id_type=MESH)

    loads = [
        pltpu.make_async_copy(src, dst, in_sem.at[i])
        for i, (src, dst) in enumerate(
            ((points, pts), (rhs, rh), (node_basis, nb), (leaf_basis, lb), (group_basis, gb))
        )
    ]
    for load in loads:
        load.start()

    flat[...] = jnp.zeros((128, 128), f32)
    flat[0:LD, 0 : 2 * NEAR + 1] = live[...].astype(f32)
    alive = flat[...].T[0:16]
    lt[...] = alive
    bias[0] = mask_table(alive, 0)

    skeleton = node_skel[...]
    leaf = skeleton // RANK
    place = lax.rem(skeleton, RANK)
    hot = (rows_of((RANK, RANK)) == place).astype(bf16)
    table = dot(leaf_skel[...].astype(f32).astype(bf16), hot)
    within = jnp.sum(jnp.where(rows_of((LD, RANK)) == leaf, table, 0.0), axis=0, keepdims=True)
    target = leaf.astype(f32) * LEAF + within
    row256 = rows_of((LEAF, RANK)).astype(f32)
    loads[0].wait()

    def pick(t, total):
        hot = (row256 == target - t.astype(f32) * LEAF).astype(bf16)
        cols = pl.ds(pl.multiple_of(t * LEAF, LEAF), LEAF)
        return total + dot(pieces(pts[:, cols]), hot)

    node_pts = thirds(lax.fori_loop(0, LD, pick, jnp.zeros((3 * D, RANK), f32)))
    hot = (rows_of((RANK, RANK)) + l * RANK == group_skel[...]).astype(bf16)
    px[x, 0:D, :] = node_pts
    px[x, D : 2 * D, :] = thirds(dot(pieces(node_pts), hot))
    ty[y] = node_pts

    pl.semaphore_wait(barrier, N_LEAF + N_GRP - 2)

    sends = []

    def send(src, dst, send_sem, recv_sem, device):
        copy = pltpu.make_async_remote_copy(
            src_ref=src, dst_ref=dst, send_sem=send_sem, recv_sem=recv_sem, device_id=device, device_id_type=MESH
        )
        copy.start()
        sends.append(copy)
        return copy

    def to_leaf(src_of, dst_of, send_sem, recv_sem):
        return [
            send(src_of(leaf_peer(k)), dst_of(k), send_sem.at[k - 1], recv_sem.at[k - 1], (g, leaf_peer(k)))
            for k in range(1, N_LEAF)
        ]

    def to_grp(src, dst, send_sem, recv_sem):
        return [
            send(src, dst, send_sem.at[k - 1], recv_sem.at[k - 1], (grp_peer(k), l)) for k in range(1, N_GRP)
        ]

    def to_x(src, dst, send_sem, recv_sem):
        return [send(src, dst, send_sem.at[k - 1], recv_sem.at[k - 1], (g, x_peer(k))) for k in range(1, SIDE)]

    def to_y(src_of, dst_of, send_sem, recv_sem):
        return [
            send(src_of(k), dst_of(k), send_sem.at[k - 1], recv_sem.at[k - 1], (g, y_peer(k))) for k in range(1, SIDE)
        ]

    def to_sides(src_of, dst_of, send_sem, recv_sem):
        return [
            send(src_of(side), dst_of(side), send_sem.at[side], recv_sem.at[side], (g, leaf_peer(k)))
            for side, k in ((0, 1), (1, N_LEAF - 1))
        ]

    def eight(i):
        return pl.ds(pl.multiple_of(i * 8, 8), 8)

    def edge(side):
        return pl.ds((LD - 2) * LEAF if side == 0 else 0, 2 * LEAF)

    x_pts = to_x(px.at[x], px.at[x], xs1, xr1)
    halo_live = to_sides(lambda side: lt, lambda side: hl.at[side], hs1, hr1)
    halo_pts = to_sides(lambda side: pts.at[:, edge(side)], lambda side: hp.at[side], hs2, hr2)
    y_pts = to_y(lambda k: ty.at[y], lambda k: ty.at[y], ys1, yr1)

    for load in loads[1:]:
        load.wait()
    wr[...] = jnp.zeros((256, 256), f32)

    def up(t, carry):
        rows = pl.ds(pl.multiple_of(t * LEAF, LEAF), LEAF)
        r = jnp.concatenate(split(rh[rows, :]), axis=1)
        R[pl.ds(pl.multiple_of((t + NEAR) * LEAF, LEAF), LEAF), :] = r
        basis = jnp.concatenate(split(lb[rows, :]), axis=1)
        inner = nb[pl.ds(pl.multiple_of(t * RANK, RANK), RANK), :]
        inner_row = jnp.concatenate(split(inner), axis=1)
        w = halves(dot(basis, jnp.concatenate([inner_row, inner_row], axis=0)))
        WW[rows, :] = jnp.concatenate(split(w), axis=1)
        high, low = split(inner.T)
        flat_w = lax.dot_general(
            jnp.concatenate([jnp.concatenate([high, high], axis=1), jnp.concatenate([low, low], axis=1)], axis=0),
            basis, NT, preferred_element_type=f32,
        )
        wr[...] += dot(jnp.concatenate(split(flat_w[:128] + flat_w[128:]), axis=0), r)
        return carry

    lax.fori_loop(0, LD, up, 0)
    node_coef = halves(wr[0:128, :] + wr[128:256, :])
    ctp[...] = mm3(node_coef.T, gb[...])
    sum_coef = to_leaf(lambda p: ctp.at[eight(p)], lambda k: gcs.at[k - 1], s1, r1)
    src_c[x] = node_coef
    for copy in x_pts:
        copy.wait_recv()
    gpy[...] = px[0, D:, :] + px[1, D:, :] + px[2, D:, :] + px[3, D:, :]
    y_sum = to_y(lambda k: gpy, lambda k: py.at[k - 1], ys2, yr2)
    x_coef = to_x(src_c.at[x], src_c.at[x], xs3, xr3)
    halo_rhs = to_sides(lambda side: rh.at[edge(side)], lambda side: hr.at[side], hs3, hr3)

    diagonal = rows_of((LEAF, LEAF)) == lax.broadcasted_iota(jnp.int32, (LEAF, LEAF), 1)
    eye = diagonal.astype(f32).astype(bf16)

    def own_features(t, carry):
        cols = pl.ds(pl.multiple_of(t * LEAF, LEAF), LEAF)
        u, v = features(pts[:, cols], column(bias[0], t), one_hot(t + NEAR))
        U[cols, :] = flip(u, eye)
        VT[:, pl.ds(pl.multiple_of(t * LEAF + PAD, LEAF), LEAF)] = v
        return carry

    lax.fori_loop(0, LD, own_features, 0)

    def add_tiles(u_ref, u_row, out_ref, count, s, depth):
        rows = pl.ds(u_row, count * LEAF)
        source = pl.ds(pl.multiple_of((s + NEAR) * LEAF, LEAF), depth * LEAF)
        k_high, k_low = kernel_block(u_ref[rows, :], VT[:, source])
        out_ref[rows, :] += apply_block(k_high, k_low, R[source, :])

    def tiles(t, count, s, depth):
        add_tiles(U, pl.multiple_of(t * LEAF, LEAF), acc, count, s, depth)

    def inner_block(b):
        tiles(b * 4, 4, b * 4 - 2, 8)

    def outer_block(i, carry):
        tiles(i * 12, 4, i * 10, 6)
        return carry

    def corners(j, carry):
        tiles(j * 4 + 4, 2, j * 4, 2)
        tiles(j * 4 + 2, 2, j * 4 + 6, 2)
        return carry

    acc[...] = jnp.zeros((ROWS, NRHS), f32)

    for copy in halo_live + halo_pts:
        copy.wait_recv()
    bias[1] = mask_table(hl[0], -N_LEAF)
    bias[2] = mask_table(hl[1], N_LEAF)
    for side in range(2):
        for i in range(2):
            cols = slice(i * LEAF, (i + 1) * LEAF)
            t = i + LD - 2 if side == 0 else i
            s = i - 2 if side == 0 else i + LD
            u, v = features(hp[side, :, cols], column(bias[1 + side], t), one_hot(s + NEAR))
            UH[side, cols, :] = flip(u, eye)
            VT[:, pl.ds((s + NEAR) * LEAF, LEAF)] = v
    accH[...] = jnp.zeros((2, 2 * LEAF, NRHS), f32)
    add_tiles(UH.at[1], 0, accH.at[1], 2, LD - 4, 4)
    add_tiles(UH.at[0], 0, accH.at[0], 2, 2, 2)
    halo_part = to_sides(lambda side: accH.at[1 - side], lambda side: hpart.at[side], hs4, hr4)

    inner_block(1)

    for copy in y_sum:
        copy.wait_recv()
    gall[g] = gpy[...] + py[0] + py[1] + py[2]
    all_pts = to_grp(gall.at[g], gall.at[g], gs1, gr1)
    for copy in sum_coef:
        copy.wait_recv()
    total = ctp[eight(l), :]
    for k in range(N_LEAF - 1):
        total = total + gcs[k]
    fmine[...] = total
    gc_out = to_grp(fmine, gc.at[g], gs2, gr2)
    gc[g] = jnp.zeros((8, 128), f32)

    for copy in y_pts + x_coef:
        copy.wait_recv()
    us, vs, rs = [], [], []
    for i in range(SIDE):
        u_col = base_u()
        for j in range(SIDE):
            close = jnp.abs(SIDE * x + i - SIDE * j - y) < 2
            u_col = u_col + jnp.where(rows_of((D, 1)) == MASK + j, jnp.where(close, DEAD, 0.0), 0.0)
        us.append(features(ty[i], u_col, None)[0].T)
        vs.append(features(px[i, 0:D, :], None, one_hot(i))[1])
        rs.append(jnp.concatenate(split(src_c[i]), axis=1))
    k_high, k_low = kernel_block(jnp.concatenate(us, axis=0), jnp.concatenate(vs, axis=1))
    field = apply_block(k_high, k_low, jnp.concatenate(rs, axis=0))
    for i in range(SIDE):
        part[i] = field[i * 128 : (i + 1) * 128]
    y_field = to_y(lambda k: part.at[lax.rem(y + k, SIDE)], lambda k: fr.at[k - 1], ys4, yr4)

    inner_block(2)

    for copy in gc_out + all_pts:
        copy.wait_recv()
    u_own = features(gall[g], base_u(), None)[0].T
    v_all = jnp.concatenate([features(gall[h], None, base_v())[1] for h in range(N_GRP)], axis=1)
    k_high, k_low = kernel_block(u_own, v_all)
    columns = jnp.concatenate([gc[h] for h in range(N_GRP)], axis=1)
    c_high = columns.astype(bf16).astype(f32)
    both = jnp.concatenate([c_high, columns - c_high], axis=0).astype(bf16)
    mine = lax.dot_general(both, k_high, NT, preferred_element_type=f32)
    mine += lax.dot_general(both, k_low, NT, preferred_element_type=f32)
    ft[eight(l), :] = mine[0:8] + mine[8:16]
    field_out = to_leaf(lambda p: ft.at[eight(l)], lambda k: ft.at[eight(l)], s2, r2)

    lax.fori_loop(0, 2, outer_block, 0)
    lax.fori_loop(0, 3, corners, 0)

    for side in range(2):
        halo_rhs[side].wait_recv()
        s = -2 if side == 0 else LD
        for i in range(2):
            r = jnp.concatenate(split(hr[side, i * LEAF : (i + 1) * LEAF, :]), axis=1)
            R[pl.ds((s + i + NEAR) * LEAF, LEAF), :] = r
    tiles(2, 2, -2, 2)
    tiles(12, 4, LD, 2)
    for copy in halo_part:
        copy.wait_recv()
    acc[edge(1), :] += hpart[0]
    acc[edge(0), :] += hpart[1]

    for copy in y_field + field_out:
        copy.wait_recv()
    node_field = part[y] + fr[0] + fr[1] + fr[2] + mm3(gb[...], ft[...].T)
    row = jnp.concatenate(split(node_field), axis=1)
    both = jnp.concatenate([row, row], axis=0)
    stores = []
    for i in range(4):
        rows = pl.ds(i * 1024, 1024)
        acc[rows, :] += halves(dot(WW[rows, :], both))
        store = pltpu.make_async_copy(acc.at[rows], out.at[rows], out_sem.at[i])
        store.start()
        stores.append(store)
    for copy in sends:
        copy.wait_send()
    for store in stores:
        store.wait()


def per_device(
    points, rhs, leaf_basis, leaf_skeleton, node_basis, node_skeleton, group_basis, group_skeleton, near_live
):
    any_ = pl.BlockSpec(memory_space=pl.ANY)
    vmem = pl.BlockSpec(memory_space=pltpu.VMEM)
    V = pltpu.VMEM
    ext = ROWS + 2 * PAD
    scratch = [
        V((D, ROWS), f32), V((ROWS, NRHS), f32), V((ROWS, RANK), f32), V((LD * RANK, RANK), f32), V((RANK, RANK), f32),
        V((ROWS, 256), bf16), V((256, ext), bf16), V((ext, 256), bf16), V((ROWS, 256), bf16), V((ROWS, NRHS), f32),
        V((3, D, 128), f32), V((256, 256), f32), V((16, 128), f32), V((128, 128), f32),
        V((SIDE, 2 * D, 128), f32), V((SIDE, D, 128), f32), V((D, 128), f32), V((SIDE - 1, D, 128), f32),
        V((N_GRP, D, 128), f32), V((128, 128), f32), V((SIDE, 128, 128), f32), V((128, 128), f32),
        V((N_LEAF - 1, 8, 128), f32), V((N_GRP, 8, 128), f32), V((8, 128), f32), V((128, 128), f32),
        V((SIDE, 128, 128), f32), V((SIDE - 1, 128, 128), f32),
        V((2, D, 2 * LEAF), f32), V((2, 16, 128), f32), V((2, 2 * LEAF, NRHS), f32), V((2, 2 * LEAF, 256), bf16),
        V((2, 2 * LEAF, NRHS), f32), V((2, 2 * LEAF, NRHS), f32),
    ]
    counts = (5, 4, 3, 3, 3, 3, 3, 3, 3, 3, 3, 3, 7, 7, 7, 7, 15, 15, 15, 15, 2, 2, 2, 2, 2, 2, 2, 2)
    scratch += [pltpu.SemaphoreType.DMA((n,)) for n in counts]
    return pl.pallas_call(
        body,
        out_shape=jax.ShapeDtypeStruct((ROWS, NRHS), f32),
        in_specs=[any_] * 5 + [vmem] * 4,
        out_specs=any_,
        scratch_shapes=scratch,
        compiler_params=pltpu.CompilerParams(
            collective_id=0, has_side_effects=True, vmem_limit_bytes=56 * 1024 * 1024
        ),
    )(
        points.T, rhs, leaf_basis.reshape(ROWS, RANK), node_basis.reshape(LD * RANK, RANK),
        group_basis.reshape(RANK, RANK), leaf_skeleton, node_skeleton, group_skeleton, near_live,
    )


def solution(mesh):
    return jax.shard_map(
        per_device,
        mesh=mesh,
        in_specs=(
            P(("grp", "leaf"), None),
            P(("grp", "leaf"), None),
            P(("grp", "leaf"), None, None),
            P(("grp", "leaf"), None),
            P(("grp", "leaf"), None, None),
            P(("grp", "leaf"), None),
            P("grp", "leaf", None),
            P("grp", None),
            P(("grp", "leaf"), None),
        ),
        out_specs=P(("grp", "leaf"), None),
        check_vma=False,
    )
```

time: 76.5 us -> 48.5 us (0.63)
  Pallas kernels: 70.1 us -> 45.3 us
  local copies, waits for them, and re-layouts: 6.2 us -> 3.05 us
    pallas_call x1, Pallas kernels: 70.1 us -> 45.3 us  [per_device(): pl.pallas_call(body, out_shape=jax.ShapeDtypeStruct((ROWS, NRHS), f32), i...]
    unnamed x2 -> x1, local copies, waits for them, and re-layouts: 6.2 us -> 3.05 us
where the time goes in v2:
time: 48.5 us; the launch traced here: 48.4 us
  Pallas kernels  45.3 us (93%)
  local copies, waits for them, and re-layouts  3.05 us (6%)
    pallas_call x1, Pallas kernels, per_device(): pl.pallas_call(body, out_shape=jax.ShapeDtypeStruct((ROWS, NRHS), f32), i...  45.3 us
    unnamed x1, local copies, waits for them, and re-layouts  3.05 us

profile of v2, /device:TPU:1, one launch (start us, length us, event | category | flops | bytes accessed | tf_op | source)
XLA Modules:
  0.0 48.4 jit_solution(3614797813372365328)
XLA Ops:
  0.0 45.3 %shard_map.91 = f32[4096,128]{1,0:T(8,128)} custom-call(f32[64,4096]{1,0:T(8,128)} %bitcast.5, f32[4096,128]{1,0:T(8,128)} %rhs.1, f32[4096,128]{1,0:T(8,128)} %bitcast.4, f32[2048,128]{1,0:T(8,128)} %bitcast.6, f32[128,128]{1,0:T(8,128)} %bitcast.7, s32[16,128]{1,0:T(8,128)} %leaf_skel.1, s32[1,128]{1,0:T(1,128)} %node_skel.1, s32[1,128]{1,0:T(1,128)} %group_skel.1, ...), custom_call_target="tpu_custom_call" | custom-call | tf_op jit(solution)/shard_map/pallas_call | solution.py:435
  45.3 3.0 %copy.11 = f32[4096,128]{1,0:T(8,128)} copy(f32[4096,128]{1,0:T(8,128)} %shard_map.91) | data formatting | bytes 4194304

commit v3 on v2

--- a/solution.py
+++ b/solution.py
@@ -192,59 +192,22 @@
         cols = pl.ds(pl.multiple_of(t * LEAF, LEAF), LEAF)
         return total + dot(pieces(pts[:, cols]), hot)
 
-    node_pts = thirds(lax.fori_loop(0, LD, pick, jnp.zeros((3 * D, RANK), f32)))
+    node_pts = thirds(lax.fori_loop(0, LD, pick, jnp.zeros((3 * D, RANK), f32), unroll=4))
     hot = (rows_of((RANK, RANK)) + l * RANK == group_skel[...]).astype(bf16)
     px[x, 0:D, :] = node_pts
     px[x, D : 2 * D, :] = thirds(dot(pieces(node_pts), hot))
     ty[y] = node_pts
 
-    pl.semaphore_wait(barrier, N_LEAF + N_GRP - 2)
-
-    sends = []
-
-    def send(src, dst, send_sem, recv_sem, device):
-        copy = pltpu.make_async_remote_copy(
-            src_ref=src, dst_ref=dst, send_sem=send_sem, recv_sem=recv_sem, device_id=device, device_id_type=MESH
-        )
-        copy.start()
-        sends.append(copy)
-        return copy
-
-    def to_leaf(src_of, dst_of, send_sem, recv_sem):
-        return [
-            send(src_of(leaf_peer(k)), dst_of(k), send_sem.at[k - 1], recv_sem.at[k - 1], (g, leaf_peer(k)))
-            for k in range(1, N_LEAF)
-        ]
-
-    def to_grp(src, dst, send_sem, recv_sem):
-        return [
-            send(src, dst, send_sem.at[k - 1], recv_sem.at[k - 1], (grp_peer(k), l)) for k in range(1, N_GRP)
-        ]
-
-    def to_x(src, dst, send_sem, recv_sem):
-        return [send(src, dst, send_sem.at[k - 1], recv_sem.at[k - 1], (g, x_peer(k))) for k in range(1, SIDE)]
-
-    def to_y(src_of, dst_of, send_sem, recv_sem):
-        return [
-            send(src_of(k), dst_of(k), send_sem.at[k - 1], recv_sem.at[k - 1], (g, y_peer(k))) for k in range(1, SIDE)
-        ]
-
-    def to_sides(src_of, dst_of, send_sem, recv_sem):
-        return [
-            send(src_of(side), dst_of(side), send_sem.at[side], recv_sem.at[side], (g, leaf_peer(k)))
-            for side, k in ((0, 1), (1, N_LEAF - 1))
-        ]
-
-    def eight(i):
-        return pl.ds(pl.multiple_of(i * 8, 8), 8)
-
-    def edge(side):
-        return pl.ds((LD - 2) * LEAF if side == 0 else 0, 2 * LEAF)
-
-    x_pts = to_x(px.at[x], px.at[x], xs1, xr1)
-    halo_live = to_sides(lambda side: lt, lambda side: hl.at[side], hs1, hr1)
-    halo_pts = to_sides(lambda side: pts.at[:, edge(side)], lambda side: hp.at[side], hs2, hr2)
-    y_pts = to_y(lambda k: ty.at[y], lambda k: ty.at[y], ys1, yr1)
+    diagonal = rows_of((LEAF, LEAF)) == lax.broadcasted_iota(jnp.int32, (LEAF, LEAF), 1)
+    eye = diagonal.astype(f32).astype(bf16)
+
+    def own_features(t, carry):
+        cols = pl.ds(pl.multiple_of(t * LEAF, LEAF), LEAF)
+        u, v = features(pts[:, cols], column(bias[0], t), one_hot(t + NEAR))
+        U[cols, :] = flip(u, eye)
+        VT[:, pl.ds(pl.multiple_of(t * LEAF + PAD, LEAF), LEAF)] = v
+        return carry
+
 
     for load in loads[1:]:
         load.wait()
@@ -267,29 +230,77 @@
         wr[...] += dot(jnp.concatenate(split(flat_w[:128] + flat_w[128:]), axis=0), r)
         return carry
 
-    lax.fori_loop(0, LD, up, 0)
+    lax.fori_loop(0, LD // 2, up, 0, unroll=4)
+    pl.semaphore_wait(barrier, N_LEAF + N_GRP - 2)
+
+    sends = []
+
+    def send(src, dst, send_sem, recv_sem, device):
+        copy = pltpu.make_async_remote_copy(
+            src_ref=src, dst_ref=dst, send_sem=send_sem, recv_sem=recv_sem, device_id=device, device_id_type=MESH
+        )
+        copy.start()
+        sends.append(copy)
+        return copy
+
+    def to_leaf(src_of, dst_of, send_sem, recv_sem):
+        return [
+            send(src_of(leaf_peer(k)), dst_of(k), send_sem.at[k - 1], recv_sem.at[k - 1], (g, leaf_peer(k)))
+            for k in range(1, N_LEAF)
+        ]
+
+    def to_grp(src, dst, send_sem, recv_sem):
+        return [
+            send(src, dst, send_sem.at[k - 1], recv_sem.at[k - 1], (grp_peer(k), l)) for k in range(1, N_GRP)
+        ]
+
+    def to_x(src, dst, send_sem, recv_sem, others):
+        result, beside = [], []
+        for k in (1, 3, 2):
+            result.append(send(src, dst, send_sem.at[k - 1], recv_sem.at[k - 1], (g, x_peer(k))))
+            if others:
+                beside.append(others.pop(0)())
+        beside += [other() for other in others]
+        return result, beside
+
+    def to_y(src_of, dst_of, send_sem, recv_sem):
+        return [
+            send(src_of(k), dst_of(k), send_sem.at[k - 1], recv_sem.at[k - 1], (g, y_peer(k))) for k in (1, 3, 2)
+        ]
+
+    def to_sides(src_of, dst_of, send_sem, recv_sem):
+        return [
+            functools.partial(
+                send, src_of(side), dst_of(side), send_sem.at[side], recv_sem.at[side], (g, leaf_peer(k))
+            )
+            for side, k in ((0, 1), (1, N_LEAF - 1))
+        ]
+
+    def eight(i):
+        return pl.ds(pl.multiple_of(i * 8, 8), 8)
+
+    def edge(side):
+        return pl.ds((LD - 2) * LEAF if side == 0 else 0, 2 * LEAF)
+
+    def send_rhs(i):
+        def rows(side):
+            return pl.ds(((LD - 2 if side == 0 else 0) + i) * LEAF, LEAF)
+
+        return to_sides(
+            lambda side: rhs.at[rows(side)], lambda side: hr.at[side, pl.ds(i * LEAF, LEAF)], hs3.at[i], hr3.at[i]
+        )
+
+    x_pts, _ = to_x(px.at[x], px.at[x], xs1, xr1, [])
+    y_pts = to_y(lambda k: ty.at[y], lambda k: ty.at[y], ys1, yr1)
+    lax.fori_loop(LD // 2, LD, up, 0, unroll=4)
     node_coef = halves(wr[0:128, :] + wr[128:256, :])
     ctp[...] = mm3(node_coef.T, gb[...])
     sum_coef = to_leaf(lambda p: ctp.at[eight(p)], lambda k: gcs.at[k - 1], s1, r1)
     src_c[x] = node_coef
-    for copy in x_pts:
-        copy.wait_recv()
-    gpy[...] = px[0, D:, :] + px[1, D:, :] + px[2, D:, :] + px[3, D:, :]
-    y_sum = to_y(lambda k: gpy, lambda k: py.at[k - 1], ys2, yr2)
-    x_coef = to_x(src_c.at[x], src_c.at[x], xs3, xr3)
-    halo_rhs = to_sides(lambda side: rh.at[edge(side)], lambda side: hr.at[side], hs3, hr3)
-
-    diagonal = rows_of((LEAF, LEAF)) == lax.broadcasted_iota(jnp.int32, (LEAF, LEAF), 1)
-    eye = diagonal.astype(f32).astype(bf16)
-
-    def own_features(t, carry):
-        cols = pl.ds(pl.multiple_of(t * LEAF, LEAF), LEAF)
-        u, v = features(pts[:, cols], column(bias[0], t), one_hot(t + NEAR))
-        U[cols, :] = flip(u, eye)
-        VT[:, pl.ds(pl.multiple_of(t * LEAF + PAD, LEAF), LEAF)] = v
-        return carry
-
-    lax.fori_loop(0, LD, own_features, 0)
+    halo_pts = to_sides(lambda side: pts.at[:, edge(side)], lambda side: hp.at[side], hs2, hr2)
+    halo_live = to_sides(lambda side: lt, lambda side: hl.at[side], hs1, hr1)
+    x_coef, halo_pts = to_x(src_c.at[x], src_c.at[x], xs3, xr3, halo_pts + halo_live)
+    lax.fori_loop(0, LD, own_features, 0, unroll=4)
 
     def add_tiles(u_ref, u_row, out_ref, count, s, depth):
         rows = pl.ds(u_row, count * LEAF)
@@ -314,7 +325,30 @@
 
     acc[...] = jnp.zeros((ROWS, NRHS), f32)
 
-    for copy in halo_live + halo_pts:
+    lax.fori_loop(0, 1, outer_block, 0)
+    for copy in x_pts:
+        copy.wait_recv()
+    gpy[...] = px[0, D:, :] + px[1, D:, :] + px[2, D:, :] + px[3, D:, :]
+    y_sum = to_y(lambda k: gpy, lambda k: py.at[k - 1], ys2, yr2)
+    halo_rhs = [start() for start in send_rhs(1)]
+    inner_block(1)
+
+    for copy in y_sum:
+        copy.wait_recv()
+    gall[g] = gpy[...] + py[0] + py[1] + py[2]
+    all_pts = to_grp(gall.at[g], gall.at[g], gs1, gr1)
+    for copy in sum_coef:
+        copy.wait_recv()
+    total = ctp[eight(l), :]
+    for k in range(N_LEAF - 1):
+        total = total + gcs[k]
+    fmine[...] = total
+    gc_out = to_grp(fmine, gc.at[g], gs2, gr2)
+    gc[g] = jnp.zeros((8, 128), f32)
+
+    halo_rhs += [start() for start in send_rhs(0)]
+
+    for copy in halo_pts:
         copy.wait_recv()
     bias[1] = mask_table(hl[0], -N_LEAF)
     bias[2] = mask_table(hl[1], N_LEAF)
@@ -329,22 +363,16 @@
     accH[...] = jnp.zeros((2, 2 * LEAF, NRHS), f32)
     add_tiles(UH.at[1], 0, accH.at[1], 2, LD - 4, 4)
     add_tiles(UH.at[0], 0, accH.at[0], 2, 2, 2)
-    halo_part = to_sides(lambda side: accH.at[1 - side], lambda side: hpart.at[side], hs4, hr4)
-
-    inner_block(1)
-
-    for copy in y_sum:
-        copy.wait_recv()
-    gall[g] = gpy[...] + py[0] + py[1] + py[2]
-    all_pts = to_grp(gall.at[g], gall.at[g], gs1, gr1)
-    for copy in sum_coef:
-        copy.wait_recv()
-    total = ctp[eight(l), :]
-    for k in range(N_LEAF - 1):
-        total = total + gcs[k]
-    fmine[...] = total
-    gc_out = to_grp(fmine, gc.at[g], gs2, gr2)
-    gc[g] = jnp.zeros((8, 128), f32)
+    def send_part(i):
+        rows = pl.ds(i * LEAF, LEAF)
+        return [
+            start()
+            for start in to_sides(
+                lambda side: accH.at[1 - side, rows], lambda side: hpart.at[side, rows], hs4.at[i], hr4.at[i]
+            )
+        ]
+
+    halo_part = send_part(0)
 
     for copy in y_pts + x_coef:
         copy.wait_recv()
@@ -361,8 +389,6 @@
     field = apply_block(k_high, k_low, jnp.concatenate(rs, axis=0))
     for i in range(SIDE):
         part[i] = field[i * 128 : (i + 1) * 128]
-    y_field = to_y(lambda k: part.at[lax.rem(y + k, SIDE)], lambda k: fr.at[k - 1], ys4, yr4)
-
     inner_block(2)
 
     for copy in gc_out + all_pts:
@@ -378,11 +404,15 @@
     ft[eight(l), :] = mine[0:8] + mine[8:16]
     field_out = to_leaf(lambda p: ft.at[eight(l)], lambda k: ft.at[eight(l)], s2, r2)
 
-    lax.fori_loop(0, 2, outer_block, 0)
-    lax.fori_loop(0, 3, corners, 0)
-
+    y_field = to_y(lambda k: part.at[lax.rem(y + k, SIDE)], lambda k: fr.at[k - 1], ys4, yr4)
+    halo_part += send_part(1)
+
+    lax.fori_loop(1, 2, outer_block, 0)
+    lax.fori_loop(0, 3, corners, 0, unroll=3)
+
+    for copy in halo_rhs:
+        copy.wait_recv()
     for side in range(2):
-        halo_rhs[side].wait_recv()
         s = -2 if side == 0 else LD
         for i in range(2):
             r = jnp.concatenate(split(hr[side, i * LEAF : (i + 1) * LEAF, :]), axis=1)
@@ -430,8 +460,8 @@
         V((2, D, 2 * LEAF), f32), V((2, 16, 128), f32), V((2, 2 * LEAF, NRHS), f32), V((2, 2 * LEAF, 256), bf16),
         V((2, 2 * LEAF, NRHS), f32), V((2, 2 * LEAF, NRHS), f32),
     ]
-    counts = (5, 4, 3, 3, 3, 3, 3, 3, 3, 3, 3, 3, 7, 7, 7, 7, 15, 15, 15, 15, 2, 2, 2, 2, 2, 2, 2, 2)
-    scratch += [pltpu.SemaphoreType.DMA((n,)) for n in counts]
+    counts = (5, 4, 3, 3, 3, 3, 3, 3, 3, 3, 3, 3, 7, 7, 7, 7, 15, 15, 15, 15, 2, 2, 2, 2, (2, 2), (2, 2), (2, 2), (2, 2))
+    scratch += [pltpu.SemaphoreType.DMA(n if isinstance(n, tuple) else (n,)) for n in counts]
     return pl.pallas_call(
         body,
         out_shape=jax.ShapeDtypeStruct((ROWS, NRHS), f32),

time: 48.5 us -> 44.6 us (0.920)
  Pallas kernels: 45.3 us -> 41.4 us
    pallas_call x1, Pallas kernels: 45.3 us -> 41.4 us  [per_device(): pl.pallas_call(body, out_shape=jax.ShapeDtypeStruct((ROWS, NRHS), f32), i...]
where the time goes in v3:
time: 44.6 us; the launch traced here: 44.4 us
  Pallas kernels  41.4 us (93%)
  local copies, waits for them, and re-layouts  3.05 us (7%)
    pallas_call x1, Pallas kernels, per_device(): pl.pallas_call(body, out_shape=jax.ShapeDtypeStruct((ROWS, NRHS), f32), i...  41.4 us
    unnamed x1, local copies, waits for them, and re-layouts  3.05 us

profile of v3, /device:TPU:1, one launch (start us, length us, event | category | flops | bytes accessed | tf_op | source)
XLA Modules:
  0.0 44.4 jit_solution(14769558885128040209)
XLA Ops:
  0.0 41.4 %shard_map.91 = f32[4096,128]{1,0:T(8,128)} custom-call(f32[64,4096]{1,0:T(8,128)} %bitcast.5, f32[4096,128]{1,0:T(8,128)} %rhs.1, f32[4096,128]{1,0:T(8,128)} %bitcast.4, f32[2048,128]{1,0:T(8,128)} %bitcast.6, f32[128,128]{1,0:T(8,128)} %bitcast.7, s32[16,128]{1,0:T(8,128)} %leaf_skel.1, s32[1,128]{1,0:T(1,128)} %node_skel.1, s32[1,128]{1,0:T(1,128)} %group_skel.1, ...), custom_call_target="tpu_custom_call" | custom-call | tf_op jit(solution)/shard_map/pallas_call | solution.py:465
  41.4 3.0 %copy.11 = f32[4096,128]{1,0:T(8,128)} copy(f32[4096,128]{1,0:T(8,128)} %shard_map.91) | data formatting | bytes 4194304

commit v4 on v3

--- a/solution.py
+++ b/solution.py
@@ -389,6 +389,7 @@
     field = apply_block(k_high, k_low, jnp.concatenate(rs, axis=0))
     for i in range(SIDE):
         part[i] = field[i * 128 : (i + 1) * 128]
+    y_field = to_y(lambda k: part.at[lax.rem(y + k, SIDE)], lambda k: fr.at[k - 1], ys4, yr4)
     inner_block(2)
 
     for copy in gc_out + all_pts:
@@ -404,7 +405,6 @@
     ft[eight(l), :] = mine[0:8] + mine[8:16]
     field_out = to_leaf(lambda p: ft.at[eight(l)], lambda k: ft.at[eight(l)], s2, r2)
 
-    y_field = to_y(lambda k: part.at[lax.rem(y + k, SIDE)], lambda k: fr.at[k - 1], ys4, yr4)
     halo_part += send_part(1)
 
     lax.fori_loop(1, 2, outer_block, 0)

time: 44.6 us -> 44.2 us (level)
  Pallas kernels: 41.4 us -> 40.9 us
    pallas_call x1, Pallas kernels: 41.4 us -> 40.9 us  [per_device(): pl.pallas_call(body, out_shape=jax.ShapeDtypeStruct((ROWS, NRHS), f32), i...]
where the time goes in v4:
time: 44.2 us; the launch traced here: 44 us
  Pallas kernels  40.9 us (93%)
  local copies, waits for them, and re-layouts  3.05 us (7%)
    pallas_call x1, Pallas kernels, per_device(): pl.pallas_call(body, out_shape=jax.ShapeDtypeStruct((ROWS, NRHS), f32), i...  40.9 us
    unnamed x1, local copies, waits for them, and re-layouts  3.05 us

profile of v4, /device:TPU:1, one launch (start us, length us, event | category | flops | bytes accessed | tf_op | source)
XLA Modules:
  0.0 44.0 jit_solution(4551389913868123540)
XLA Ops:
  0.0 40.9 %shard_map.91 = f32[4096,128]{1,0:T(8,128)} custom-call(f32[64,4096]{1,0:T(8,128)} %bitcast.5, f32[4096,128]{1,0:T(8,128)} %rhs.1, f32[4096,128]{1,0:T(8,128)} %bitcast.4, f32[2048,128]{1,0:T(8,128)} %bitcast.6, f32[128,128]{1,0:T(8,128)} %bitcast.7, s32[16,128]{1,0:T(8,128)} %leaf_skel.1, s32[1,128]{1,0:T(1,128)} %node_skel.1, s32[1,128]{1,0:T(1,128)} %group_skel.1, ...), custom_call_target="tpu_custom_call" | custom-call | tf_op jit(solution)/shard_map/pallas_call | solution.py:465
  40.9 3.0 %copy.11 = f32[4096,128]{1,0:T(8,128)} copy(f32[4096,128]{1,0:T(8,128)} %shard_map.91) | data formatting | bytes 4194304
